TPU v7x, 256 devices: a whole 4x4x8 slice. The times are simulated.
256 devices in a mesh: expert: 64 (over x, z, core), hidden: 4 (over y).
Axes of the slice: x: 4, y: 4, z: 8, core: 2. Of those that a mesh axis runs over, the one named last changes fastest.
Arguments:
- pixels: bfloat16 [65536, 1024], P('expert', 'hidden'), may hold values from -6 to 6
- conv_weight: float32 [9, 1024], P(None, 'hidden'), may hold values from -2.5 to 2.5
- norm_gain: float32 [1024], replicated, may hold values from 0.1 to 1.9
- router_weight: bfloat16 [1024, 64], P(None, 'expert'), may hold values from -0.375 to 0.375
- gate_weight: bfloat16 [64, 1024, 4096], P('expert', None, 'hidden'), may hold values from -0.1875 to 0.1875
- up_weight: bfloat16 [64, 1024, 4096], P('expert', None, 'hidden'), may hold values from -0.1875 to 0.1875
- down_weight: bfloat16 [64, 4096, 1024], P('expert', 'hidden'), may hold values from -0.09375 to 0.09375
- expert_ids: int32 [65536, 1], P('expert'), may hold values from 0 to 63; in each aligned block of 1024 rows (0 to 1023, 1024 to 2047, ...) at most 32 rows name the same one
- neighbours: int32 [64, 8], P('expert'), may hold values from -1 to 63, as said below
Outputs:
- block_out: bfloat16 [65536, 1024], P('expert', 'hidden')
Inputs may be any that keep to these rules, and one draw needn't show every extreme that they name: `expert_ids`: among the 1024 pixels of one tile (the rows of one device) no expert is named more than 32 times. `neighbours`: A simplified stand-in for the sphere's tile adjacency: the tiles form a grid of 16 rows by 4 columns that closes in the columns; row t lists the tiles to the north, south, west, east, northwest, northeast, southwest and southeast of tile t, and -1 stands for a place beyond the first or last grid row. Which tile stands where is arbitrary.
All inputs are finite; a program needn't handle non-finite values.
Results may differ from a plain program's by a relative error of at most 0.0055.
Values may be sent and summed in bfloat16 or wider, within the bound.
A program may use at most 128 MiB of HBM per device.

v0:
```python
import jax
import jax.numpy as jnp
from jax import lax
from jax.sharding import PartitionSpec as P

TILE_SIDE = 32


epsilon = 1e-05


def shards(
    pixels,
    conv_weight,
    norm_gain,
    router_weight,
    gate_weight,
    up_weight,
    down_weight,
    expert_ids,
    neighbours,
):
    tile_side = TILE_SIDE
    tokens_dev, width_own = pixels.shape
    experts = lax.axis_size("expert")
    capacity = max(2, 2 * tokens_dev // experts)
    tile_grid = pixels.reshape(tile_side, tile_side, width_own)
    rim_cells = jnp.concatenate(
        [
            tile_grid[0],
            tile_grid[tile_side - 1],
            tile_grid[:, 0],
            tile_grid[:, tile_side - 1],
            tile_grid[0, 0][None],
            tile_grid[0, tile_side - 1][None],
            tile_grid[tile_side - 1, 0][None],
            tile_grid[tile_side - 1, tile_side - 1][None],
        ],
        axis=0,
    )
    gathered = lax.all_gather(rim_cells, "expert", axis=0, tiled=True).reshape(
        experts, 4 * tile_side + 4, width_own
    )
    tile_table = neighbours[0]
    present = (tile_table >= 0).astype(jnp.bfloat16)
    source_tile = jnp.maximum(tile_table, 0)

    def fetch_rim(direction, first_row, row_count):
        picked = lax.dynamic_index_in_dim(gathered, source_tile[direction], 0, keepdims=False)
        return (
            lax.slice_in_dim(picked, first_row, first_row + row_count, axis=0) * present[direction]
        )

    north = fetch_rim(0, tile_side, tile_side)
    south = fetch_rim(1, 0, tile_side)
    west = fetch_rim(2, 3 * tile_side, tile_side)
    east = fetch_rim(3, 2 * tile_side, tile_side)
    corner_nw = fetch_rim(4, 4 * tile_side + 3, 1)
    corner_ne = fetch_rim(5, 4 * tile_side + 2, 1)
    corner_sw = fetch_rim(6, 4 * tile_side + 1, 1)
    corner_se = fetch_rim(7, 4 * tile_side, 1)
    upper_rim = jnp.concatenate([corner_nw, north, corner_ne], axis=0)
    lower_rim = jnp.concatenate([corner_sw, south, corner_se], axis=0)
    middle = jnp.concatenate([west[:, None], tile_grid, east[:, None]], axis=1)
    padded = jnp.concatenate([upper_rim[None], middle, lower_rim[None]], axis=0).astype(jnp.float32)
    mixed = tile_grid.astype(jnp.float32)
    for row_off in range(3):
        for col_off in range(3):
            mixed = (
                mixed
                + conv_weight[3 * row_off + col_off]
                * padded[row_off : row_off + tile_side, col_off : col_off + tile_side]
            )
    conv_out = mixed.astype(jnp.bfloat16).reshape(tokens_dev, width_own)
    expert_of = expert_ids[:, 0]
    onehot = (expert_of[:, None] == jnp.arange(experts, dtype=jnp.int32)[None]).astype(jnp.bfloat16)
    lower_tri = (jnp.arange(tokens_dev)[:, None] > jnp.arange(tokens_dev)[None]).astype(
        jnp.bfloat16
    )
    earlier = jnp.dot(lower_tri, onehot, preferred_element_type=jnp.float32)
    slot_index = jnp.sum(earlier * onehot.astype(jnp.float32), axis=1).astype(jnp.int32)
    position = expert_of * capacity + slot_index
    whole = lax.all_gather(conv_out, "hidden", axis=1, tiled=True)
    wide_feats = whole.astype(jnp.float32)
    mean_sq = jnp.mean(wide_feats * wide_feats, axis=1, keepdims=True)
    normed = (wide_feats * lax.rsqrt(mean_sq + epsilon) * norm_gain).astype(jnp.bfloat16)
    buffer = jnp.zeros((experts * capacity, whole.shape[1]), jnp.bfloat16).at[position].set(normed)
    buffer = buffer.reshape(experts, capacity, whole.shape[1])
    received = lax.all_to_all(buffer, "expert", split_axis=0, concat_axis=0, tiled=True)
    row_count = received.shape[1]
    full_width = received.shape[2]
    row_block = received.reshape(experts * row_count, full_width)
    score = jnp.dot(row_block, router_weight, preferred_element_type=jnp.float32)
    weight = jax.nn.sigmoid(score)
    gate_act = jnp.dot(row_block, gate_weight[0], preferred_element_type=jnp.float32)
    up_act = jnp.dot(row_block, up_weight[0], preferred_element_type=jnp.float32)
    hidden = (jax.nn.silu(gate_act) * up_act * weight).astype(jnp.bfloat16)
    columns = down_weight[0]
    scattered = lax.psum_scatter(
        lax.dot_general(
            columns, hidden, (((0,), (1,)), ((), ())), preferred_element_type=jnp.float32
        ).astype(jnp.bfloat16),
        "hidden",
        scatter_dimension=0,
        tiled=True,
    ).astype(jnp.float32)
    outgoing = scattered.T.astype(jnp.bfloat16).reshape(experts, row_count, width_own)
    returned = lax.all_to_all(outgoing, "expert", split_axis=0, concat_axis=0, tiled=True)
    combined = returned.reshape(experts * capacity, width_own)[position]
    return (conv_out.astype(jnp.float32) + combined.astype(jnp.float32)).astype(jnp.bfloat16)


def solution(mesh):
    in_specs = (
        P("expert", "hidden"),
        P(None, "hidden"),
        P(),
        P(None, "expert"),
        P("expert", None, "hidden"),
        P("expert", None, "hidden"),
        P("expert", "hidden", None),
        P("expert", None),
        P("expert", None),
    )
    out_specs = P("expert", "hidden")
    return jax.shard_map(shards, mesh=mesh, in_specs=in_specs, out_specs=out_specs, check_vma=False)
```

profile of v0, /device:TPU:1, one launch (start us, length us, event | category | flops | bytes accessed | tf_op | source)
XLA Modules:
  0.0 380.2 jit_solution(7681025784083747987)
XLA Ops:
  6.5 0.0 copy-start
  6.5 0.0 all-gather.6.cloned.1.call-start
  6.5 0.9 fusion.42
  7.4 0.7 slice_bitcast_fusion
  8.2 1.0 fusion.41
  9.2 3.0 concatenate.15
  12.3 0.0 all-gather.6.cloned.1.call-update
  12.3 0.0 all-gather.4.cloned.1.call-start
  12.3 0.7 broadcast_maximum_fusion
  13.0 0.7 fusion.45
  28.2 0.7 compare_convert_fusion
  28.9 0.7 fusion.44
  29.6 1.0 fusion.43
  30.6 65.2 %all-gather.6.cloned.1.call-done = bf16[64,132,256]{2,1,0:T(8,128)(2,1)} async-done(((bf16[1,132,256]{2,1,0:T(8,128)(2,1)}), bf16[64,132,256]{2,1,0:T(8,128)(2,1)}) %all-gather.6.cloned.1.call-update) | async-done | bytes 4325392 | tf_op jit(solution)/shard_map/all_gather | solution.py:41
  95.7 3.2 fusion.31
  99.0 3.1 fusion.33
  102.2 1.3 maximum_convert_fusion
  103.5 0.0 copy-start.4
  103.5 2.7 fusion.17
  106.2 0.0 copy-start.2
  106.2 0.0 all-gather.4.cloned.1.call-update
  106.2 0.0 reduce-scatter.2.cloned.1.call-start
  106.3 0.0 copy-done.4
  106.3 0.6 fusion.15
  106.9 32.6 %all-gather.4.cloned.1.call-done = bf16[1024,1024]{1,0:T(8,128)(2,1)} async-done(((bf16[1024,256]{1,0:T(8,128)(2,1)}), bf16[1024,1024]{1,0:T(8,128)(2,1)}) %all-gather.4.cloned.1.call-update) | async-done | bytes 2097168 | tf_op jit(solution)/shard_map/all_gather | solution.py:83
  139.6 2.1 fusion
  141.7 0.0 copy-done.2
  141.7 9.0 %scatter_custom_fusion = bf16[2048,1024]{1,0:T(8,128)(2,1)} fusion(s32[1024]{0:T(1024)S(1)} %bitcast.101, bf16[1024,1024]{1,0:T(8,128)(2,1)} %all-gather.4.cloned.1.call-done, f32[1024]{0:T(1024)S(1)} %copy-done.2, f32[1024]{0:T(1024)S(1)} %add_rsqrt_fusion, bf16[]{:T(256)} %constant.32.clone.1), kind=kCustom, calls=%fused_computation.11 | custom fusion | flops 4194304 | bytes 6299650 | tf_op jit(solution)/shard_map/scatter | solution.py:87
  150.7 0.0 copy-start.3
  150.7 107.8 %all_to_all.10 = bf16[64,32,1024]{2,1,0:T(8,128)(2,1)S(1)} all-to-all(bf16[64,32,1024]{2,1,0:T(8,128)(2,1)} %bitcast.92), channel_id=1, replica_groups=mesh['expert'=64,'hidden'=4] {'expert'}, dimensions={0} | all-to-all | bytes 8388608 | tf_op jit(solution)/shard_map/all_to_all | solution.py:89
  258.5 0.0 copy-start.1
  258.5 0.0 copy-done.3
  258.5 1.2 fusion.46
  259.7 0.7 copy-done.1
  260.4 0.0 copy-done
  260.4 6.6 %fusion.9 = f32[2048,1024]{1,0:T(8,128)} fusion(bf16[2048,1024]{1,0:T(8,128)(2,1)S(1)} %bitcast.90, bf16[1,1024,1024]{2,1,0:T(8,128)(2,1)S(1)} %copy-done), kind=kOutput, calls=%fused_computation.14 | convolution fusion | flops 4294967296 | bytes 14680064 | tf_op jit(solution)/shard_map/dot_general | solution.py:95
  267.1 14.6 %convert_bitcast_fusion = bf16[1024,2048]{0,1:T(8,128)(2,1)} fusion(f32[2048,1024]{1,0:T(8,128)} %fusion.9, bf16[2048,1024]{1,0:T(8,128)(2,1)} %bitcast.91, f32[2048]{0:T(1024)S(1)} %add_divide_fusion, bf16[1,1024,1024]{2,1,0:T(8,128)(2,1)} %param.15, bf16[1,1024,1024]{2,1,0:T(8,128)(2,1)} %param.14), kind=kOutput, calls=%fused_computation.8 | convolution fusion | flops 8606711808 | bytes 20979712 | tf_op jit(solution)/shard_map/dot_general | solution.py:100
  281.7 0.0 reduce-scatter.2.cloned.1.call-update
  281.7 45.8 %reduce-scatter.2.cloned.1.call-done = bf16[256,2048]{0,1:T(8,128)(2,1)} async-done(((bf16[1024,2048]{0,1:T(8,128)(2,1)}), bf16[256,2048]{0,1:T(8,128)(2,1)}) %reduce-scatter.2.cloned.1.call-update) | async-done | bytes 1048592 | tf_op jit(solution)/shard_map/reduce_scatter | solution.py:99
  327.4 10.6 %all-to-all-start.1 = ((bf16[64,32,256]{2,1,0:T(8,128)(2,1)}), bf16[64,32,256]{2,1,0:T(8,128)(2,1)S(1)}, u32[]{:S(2)}, u32[]{:S(2)}) async-start(bf16[64,32,256]{2,1,0:T(8,128)(2,1)} %bitcast.98), calls=%async_computation.2 | async-start | bytes 2097152 | tf_op jit(solution)/shard_map/all_to_all | solution.py:108
  338.0 28.5 %all-to-all-done.1 = bf16[64,32,256]{2,1,0:T(8,128)(2,1)S(1)} async-done(((bf16[64,32,256]{2,1,0:T(8,128)(2,1)}), bf16[64,32,256]{2,1,0:T(8,128)(2,1)S(1)}, u32[]{:S(2)}, u32[]{:S(2)}) %all-to-all-start.1) | async-done | bytes 1048608 | tf_op jit(solution)/shard_map/all_to_all | solution.py:108
  366.6 5.0 %gather_fusion = bf16[1024,256]{1,0:T(8,128)(2,1)} fusion(bf16[2048,256]{1,0:T(8,128)(2,1)S(1)} %bitcast.88, s32[1024]{0:T(1024)S(1)} %broadcast_clamp_fusion), kind=kCustom, calls=%fused_computation | custom fusion | bytes 1052672 | tf_op jit(solution)/shard_map/gather | solution.py:109
  371.6 2.1 add_convert_fusion
  (10 shorter events, 0.1 us)
Async XLA Ops:
  6.5 253.9 %copy-start = (bf16[1,1024,1024]{2,1,0:T(8,128)(2,1)S(1)}, bf16[1,1024,1024]{2,1,0:T(8,128)(2,1)}, u32[]{:S(2)}) copy-start(bf16[1,1024,1024]{2,1,0:T(8,128)(2,1)} %param.13) | copy-start | bytes 6291460
  6.5 89.2 %all-gather.6.cloned.1.call-start = ((), (), s32[]{:S(2)}) async-start(), calls=%async_computation.5 | async-start | bytes 4526080 | tf_op jit(solution)/shard_map/all_gather | solution.py:41
  12.3 127.3 %all-gather.4.cloned.1.call-start = ((), (), s32[]{:S(2)}) async-start(), calls=%async_computation.3 | async-start | bytes 2621440 | tf_op jit(solution)/shard_map/all_gather | solution.py:83
  103.5 2.8 copy-start.4
  106.2 35.4 %copy-start.2 = (f32[1024]{0:T(1024)S(1)}, f32[1024]{0:T(1024)}, u32[]{:S(2)}) copy-start(f32[1024]{0:T(1024)} %param.11) | copy-start | bytes 12292
  106.2 221.2 %reduce-scatter.2.cloned.1.call-start = ((), (), s32[]{:S(2)}) async-start(), calls=%async_computation.4 | async-start | bytes 5242880 | tf_op jit(solution)/shard_map/reduce_scatter | solution.py:99
  150.7 107.8 %copy-start.3 = (bf16[1024,1]{0,1:T(2,128)(2,1)S(1)}, bf16[1024,1]{0,1:T(2,128)(2,1)}, u32[]{:S(2)}) copy-start(bf16[1024,1]{0,1:T(2,128)(2,1)} %param.12) | copy-start | bytes 6148
  258.5 1.9 copy-start.1
  327.4 39.1 %all-to-all-start.1 = ((bf16[64,32,256]{2,1,0:T(8,128)(2,1)}), bf16[64,32,256]{2,1,0:T(8,128)(2,1)S(1)}, u32[]{:S(2)}, u32[]{:S(2)}) async-start(bf16[64,32,256]{2,1,0:T(8,128)(2,1)} %bitcast.98), calls=%async_computation.2 | async-start | bytes 2097152 | tf_op jit(solution)/shard_map/all_to_all | solution.py:108
Sparse Core Ops, SparseCore 0:
  12.4 83.2 all-gather.5
  106.4 33.1 all-gather.3
  281.8 45.5 reduce-scatter.1
where the time goes:
time: 381 us; the launch traced here: 380 us
  waiting for transfers between devices  172 us (45%)
  blocking collectives  108 us (28%)
  between operations  27.8 us (7%)
  other arithmetic  24.9 us (7%)
  matrix products  23 us (6%)
  local copies, waits for them, and re-layouts  13.8 us (4%)
  starting transfers between devices  10.7 us (3%)
    all_to_all x1, blocking collectives, shards(): lax.all_to_all(buffer, 'expert', split_axis=0, concat_axis=0, tiled=True)  108 us
    all_gather x1, waiting for transfers between devices, shards(): lax.all_gather(rim_cells, 'expert', axis=0, tiled=True)  65.2 us
    reduce_scatter x1, waiting for transfers between devices, shards(): lax.psum_scatter(lax.dot_general(columns, hidden, (((0,), (1,)), ((), ())...  45.8 us
    all_gather x1, waiting for transfers between devices, shards(): whole = lax.all_gather(conv_out, 'hidden', axis=1, tiled=True)  32.6 us
    all_to_all x1, waiting for transfers between devices, shards(): lax.all_to_all(outgoing, 'expert', split_axis=0, concat_axis=0, tiled=True)  28.5 us
    dot_general x1, matrix products, shards(): lax.dot_general(columns, hidden, (((0,), (1,)), ((), ())), preferred_elem...  14.6 us
    all_to_all x1, starting transfers between devices, shards(): lax.all_to_all(outgoing, 'expert', split_axis=0, concat_axis=0, tiled=True)  10.6 us
    scatter x1, other arithmetic, shards(): jnp.zeros((experts * capacity, whole.shape[1]), jnp.bfloat16).at[position]  8.98 us
  transfers between devices with their start and end apart: 4, of which 4 were waited for; matrix products, arithmetic and copies ran while one was open for 1% of the time, Pallas kernels for 0%

commit v1 on v0

v1 whole, which is shorter than its diff:
```python
import jax
import jax.numpy as jnp
from jax import lax
from jax.experimental import pallas as pl
from jax.experimental.pallas import tpu as pltpu
from jax.sharding import PartitionSpec as P

MESH = pl.DeviceIdType.MESH
F32 = jnp.float32
BF16 = jnp.bfloat16

SIDE = 32
TOKENS = SIDE * SIDE
EXPERTS = 64
CAP = 32
OWN = 256
PARTS = 4
UNITS = 1024
WIDTH = OWN * PARTS
GROUPS = 8
BLOCKS = EXPERTS // GROUPS
HALF = BLOCKS // 2
ROWS = BLOCKS * CAP
LEFT = 8
EPSILON = 1e-05


def kernel(
    pixels,
    conv_weight,
    norm_gain,
    router,
    ids,
    table,
    gate_hbm,
    up_hbm,
    down_hbm,
    out,
    padded,
    rim_out,
    rim_in,
    pick_out,
    pick_in,
    conv,
    place_row,
    place_col,
    router_wide,
    gate_w,
    up_w,
    down_w,
    outgoing,
    rows,
    normed,
    hidden,
    partial,
    relay_dn,
    relay_up,
    sums_dn,
    sums_up,
    final,
    returned,
    total,
    weight_sem,
    send_sem,
    rim_sem,
    disp_sem,
    gat_dn,
    gat_up,
    fwd_dn,
    fwd_up,
    rel_dn,
    rel_up,
    sum_dn,
    sum_up,
    ret_sem,
):
    e = lax.axis_index("expert")
    y = lax.axis_index("hidden")
    x, z, c = lax.div(e, 16), lax.rem(lax.div(e, 2), 8), lax.rem(e, 2)
    up, dn, op = lax.rem(y + 1, 4), lax.rem(y + 3, 4), lax.rem(y + 2, 4)

    def ahead(k):
        dx, dc, dz = lax.div(k, 16), lax.rem(lax.div(k, 8), 2), lax.rem(k, 8)
        return (lax.rem(x + dx, 4) * 8 + lax.rem(z + dz, 8)) * 2 + lax.rem(c + dc, 2)

    def behind(k):
        dx, dc, dz = lax.div(k, 16), lax.rem(lax.div(k, 8), 2), lax.rem(k, 8)
        return (lax.rem(x + 4 - dx, 4) * 8 + lax.rem(z + 8 - dz, 8)) * 2 + lax.rem(c + dc, 2)

    def remote(src, dst, sent, got, target):
        return pltpu.make_async_remote_copy(
            src_ref=src,
            dst_ref=dst,
            send_sem=sent,
            recv_sem=got,
            device_id=target,
            device_id_type=MESH,
        )

    def received(dst, sem):
        remote(dst, dst, send_sem.at[0], sem, (e, up)).wait_recv()

    def sent(src, sem):
        remote(src, src, sem, rim_sem.at[0], (e, up)).wait_send()

    barrier = pltpu.get_barrier_semaphore()

    def greet(k, carry):
        pl.semaphore_signal(barrier, inc=1, device_id=(ahead(k), y), device_id_type=MESH)
        return carry

    lax.fori_loop(1, EXPERTS, greet, 0)
    pl.semaphore_signal(barrier, inc=1, device_id=(e, up), device_id_type=MESH)
    pl.semaphore_signal(barrier, inc=1, device_id=(e, dn), device_id_type=MESH)

    loads = [
        pltpu.make_async_copy(gate_hbm.at[0], gate_w, weight_sem.at[0]),
        pltpu.make_async_copy(up_hbm.at[0], up_w, weight_sem.at[1]),
        pltpu.make_async_copy(down_hbm.at[0], down_w, weight_sem.at[2]),
    ]
    for load in loads:
        load.start()

    def widen(i, carry):
        at = pl.multiple_of(i * SIDE, SIDE)
        padded[i + 1, LEFT : LEFT + SIDE, :] = pixels[pl.ds(at, SIDE), :].astype(F32)
        return carry

    lax.fori_loop(0, SIDE, widen, 0)
    rim_out[...] = jnp.zeros_like(rim_out)
    near, far = LEFT, LEFT + SIDE - 1
    for half in range(2):
        lanes = slice(128 * half, 128 * half + 128)
        at = slice(SIDE * half, SIDE * half + SIDE)
        rim_out[at, 0, :] = padded[1, near : far + 1, lanes]
        rim_out[at, 1, :] = padded[SIDE, near : far + 1, lanes]
        rim_out[at, 2, :] = padded[1 : SIDE + 1, near, lanes]
        rim_out[at, 3, :] = padded[1 : SIDE + 1, far, lanes]
    rim_out[:, 4, 0:8] = jnp.broadcast_to(table[...].astype(F32), (EXPERTS, 8))

    pl.semaphore_wait(barrier, EXPERTS - 1 + 2)

    def send_rim(k, carry):
        target = ahead(k)
        remote(
            rim_out.at[target], rim_in.at[e], send_sem.at[0], rim_sem.at[0], (target, y)
        ).start()
        return carry

    lax.fori_loop(1, EXPERTS, send_rim, 0)
    rim_in[e] = rim_out[e]

    onehot = (
        ids[...] == lax.broadcasted_iota(jnp.int32, (EXPERTS, TOKENS), 0)
    ).astype(F32)
    onehot_bf = onehot.astype(BF16)

    def places(b, carry):
        at = pl.multiple_of(b * 256, 256)
        earlier = lax.broadcasted_iota(jnp.int32, (TOKENS, 256), 0) < (
            lax.broadcasted_iota(jnp.int32, (TOKENS, 256), 1) + at
        )
        counts = jnp.dot(
            onehot_bf, earlier.astype(F32).astype(BF16), preferred_element_type=F32
        )
        own = ids[0:1, pl.ds(at, 256)]
        chosen = own == lax.broadcasted_iota(jnp.int32, (EXPERTS, 256), 0)
        slot = jnp.sum(jnp.where(chosen, counts, 0.0), axis=0, keepdims=True)
        dx = (lax.shift_right_logical(own, 4) - x + 4) & 3
        dz = ((lax.shift_right_logical(own, 1) & 7) - z + 8) & 7
        dc = ((own & 1) + c) & 1
        place = (dx * 16 + dc * 8 + dz).astype(F32) * CAP + slot
        place_row[0:1, pl.ds(at, 256)] = place
        place_col[pl.ds(at, 256), :] = jnp.broadcast_to(place, (128, 256)).T
        return carry

    lax.fori_loop(0, TOKENS // 256, places, 0)

    def widen_router(b, carry):
        at = pl.multiple_of(b * 256, 256)
        column = router[0:1, pl.ds(at, 256)].astype(F32)
        router_wide[pl.ds(at, 256), :] = jnp.broadcast_to(column, (128, 256)).T.astype(BF16)
        return carry

    lax.fori_loop(0, WIDTH // 256, widen_router, 0)

    received(rim_in.at[pl.ds(0, EXPERTS - 1)], rim_sem.at[0])
    tables = rim_in[:, 4, :]
    tile = lax.broadcasted_iota(jnp.int32, (EXPERTS, EXPERTS), 1).astype(F32)
    edges = [rim_in[:, edge, :].astype(BF16) for edge in range(4)]
    for direction, edge in enumerate((1, 0, 3, 2, 1, 1, 0, 0)):
        chosen = (tables[:, direction : direction + 1] == tile).astype(F32).astype(BF16)
        pick_out[:, direction, :] = jnp.dot(chosen, edges[edge], preferred_element_type=F32)

    def send_pick(k, carry):
        target = ahead(k)
        remote(
            pick_out.at[target], pick_in.at[e], send_sem.at[1], rim_sem.at[1], (target, y)
        ).start()
        return carry

    lax.fori_loop(1, EXPERTS, send_pick, 0)
    pick_in[e] = pick_out[e]
    received(pick_in.at[pl.ds(0, EXPERTS - 1)], rim_sem.at[1])

    for half in range(2):
        lanes = slice(128 * half, 128 * half + 128)
        at = slice(SIDE * half, SIDE * half + SIDE)
        first, last = SIDE * half, SIDE * half + SIDE - 1
        padded[0, near : far + 1, lanes] = pick_in[at, 0, :]
        padded[SIDE + 1, near : far + 1, lanes] = pick_in[at, 1, :]
        padded[1 : SIDE + 1, near - 1, lanes] = pick_in[at, 2, :]
        padded[1 : SIDE + 1, far + 1, lanes] = pick_in[at, 3, :]
        padded[0, near - 1 : near, lanes] = pick_in[last, 4:5, :]
        padded[0, far + 1 : far + 2, lanes] = pick_in[first, 5:6, :]
        padded[SIDE + 1, near - 1 : near, lanes] = pick_in[last, 6:7, :]
        padded[SIDE + 1, far + 1 : far + 2, lanes] = pick_in[first, 7:8, :]

    def convolve(i, carry):
        mixed = padded[i + 1, near : far + 1, :]
        for a in range(3):
            for b in range(3):
                tap = conv_weight[3 * a + b : 3 * a + b + 1, :]
                mixed = mixed + tap * padded[i + a, near - 1 + b : far + b, :]
        conv[pl.ds(pl.multiple_of(i * SIDE, SIDE), SIDE), :] = mixed.astype(BF16)
        return carry

    lax.fori_loop(0, SIDE, convolve, 0)
    total[...] = jnp.zeros_like(total)

    def dispatch(g):
        first = lax.broadcasted_iota(jnp.int32, (ROWS, TOKENS), 0) + g * ROWS
        chosen = (place_row[...] == first.astype(F32)).astype(F32).astype(BF16)
        block = jnp.dot(chosen, conv[...], preferred_element_type=F32).astype(BF16)
        outgoing[pl.ds(g * BLOCKS, BLOCKS)] = block.reshape(BLOCKS, CAP, OWN)

        @pl.when(g == 0)
        def _():
            pltpu.make_async_copy(outgoing.at[0], rows.at[y, 0], disp_sem.at[0]).start()

        def send(k, carry):
            remote(
                outgoing.at[k], rows.at[y, k], send_sem.at[2], disp_sem.at[g], (ahead(k), y)
            ).start()
            return carry

        lax.fori_loop(jnp.where(g == 0, 1, g * BLOCKS), (g + 1) * BLOCKS, send, 0)

    def gather(g):
        span = pl.ds(g * BLOCKS, BLOCKS)
        mine = rows.at[y, span]
        received(mine, disp_sem.at[g])
        remote(mine, mine, send_sem.at[3], gat_dn.at[g], (e, up)).start()
        remote(mine, mine, send_sem.at[4], gat_up.at[g], (e, dn)).start()

    def forward(g):
        received(rows.at[dn, pl.ds(g * BLOCKS, BLOCKS)], gat_dn.at[g])
        low = rows.at[dn, pl.ds(g * BLOCKS, HALF)]
        remote(low, low, send_sem.at[5], fwd_dn.at[g], (e, up)).start()
        received(rows.at[up, pl.ds(g * BLOCKS, BLOCKS)], gat_up.at[g])
        high = rows.at[up, pl.ds(g * BLOCKS + HALF, HALF)]
        remote(high, high, send_sem.at[6], fwd_up.at[g], (e, dn)).start()

    def expert(g):
        received(rows.at[op, pl.ds(g * BLOCKS, HALF)], fwd_dn.at[g])
        received(rows.at[op, pl.ds(g * BLOCKS + HALF, HALF)], fwd_up.at[g])
        span = pl.ds(g * BLOCKS, BLOCKS)
        squares = jnp.zeros((ROWS, 1), F32)
        for part in range(PARTS):
            wide = rows[part, span].reshape(ROWS, OWN).astype(F32)
            squares = squares + jnp.sum(wide * wide, axis=1, keepdims=True)
        scale = lax.rsqrt(squares * (1.0 / WIDTH) + EPSILON)
        for part in range(PARTS):
            wide = rows[part, span].reshape(ROWS, OWN).astype(F32)
            normed[:, part * OWN : (part + 1) * OWN] = (
                wide * scale * norm_gain[part : part + 1, :]
            ).astype(BF16)
        score = jnp.dot(normed[...], router_wide[...], preferred_element_type=F32)
        weight = 1.0 / (1.0 + jnp.exp(-score))
        weight = jnp.concatenate([weight, weight], axis=1)

        def units(n, carry):
            at = pl.ds(pl.multiple_of(n * 256, 256), 256)
            gate = jnp.dot(normed[...], gate_w[:, at], preferred_element_type=F32)
            lift = jnp.dot(normed[...], up_w[:, at], preferred_element_type=F32)
            hidden[:, at] = (gate / (1.0 + jnp.exp(-gate)) * lift * weight).astype(BF16)
            return carry

        lax.fori_loop(0, UNITS // 256, units, 0)

        def channels(part, carry):
            at = pl.ds(pl.multiple_of(part * OWN, OWN), OWN)
            result = jnp.dot(hidden[...], down_w[:, at], preferred_element_type=F32)
            partial[part, span] = result.astype(BF16).reshape(BLOCKS, CAP, OWN)
            return carry

        lax.fori_loop(0, PARTS, channels, 0)

        low, high = pl.ds(g * BLOCKS, HALF), pl.ds(g * BLOCKS + HALF, HALF)
        slot = pl.ds(g * HALF, HALF)
        remote(
            partial.at[op, low], relay_dn.at[slot], send_sem.at[7], rel_dn.at[g], (e, up)
        ).start()
        remote(
            partial.at[op, high], relay_up.at[slot], send_sem.at[8], rel_up.at[g], (e, dn)
        ).start()
        remote(
            partial.at[up, high], sums_dn.at[high], send_sem.at[9], sum_dn.at[g], (e, up)
        ).start()
        remote(
            partial.at[dn, low], sums_up.at[low], send_sem.at[10], sum_up.at[g], (e, dn)
        ).start()

    def relay(g):
        low, high = pl.ds(g * BLOCKS, HALF), pl.ds(g * BLOCKS + HALF, HALF)
        slot = pl.ds(g * HALF, HALF)
        received(relay_dn.at[slot], rel_dn.at[g])
        partial[up, low] = (partial[up, low].astype(F32) + relay_dn[slot].astype(F32)).astype(BF16)
        remote(
            partial.at[up, low], sums_dn.at[low], send_sem.at[9], sum_dn.at[g], (e, up)
        ).start()
        received(relay_up.at[slot], rel_up.at[g])
        partial[dn, high] = (
            partial[dn, high].astype(F32) + relay_up[slot].astype(F32)
        ).astype(BF16)
        remote(
            partial.at[dn, high], sums_up.at[high], send_sem.at[10], sum_up.at[g], (e, dn)
        ).start()

    def give_back(g):
        span = pl.ds(g * BLOCKS, BLOCKS)
        received(sums_dn.at[span], sum_dn.at[g])
        received(sums_up.at[span], sum_up.at[g])
        final[span] = (
            partial[y, span].astype(F32) + sums_dn[span].astype(F32) + sums_up[span].astype(F32)
        ).astype(BF16)

        @pl.when(g == 0)
        def _():
            pltpu.make_async_copy(final.at[0], returned.at[0], ret_sem.at[0]).start()

        def send(k, carry):
            remote(
                final.at[k], returned.at[k], send_sem.at[11], ret_sem.at[g], (behind(k), y)
            ).start()
            return carry

        lax.fori_loop(jnp.where(g == 0, 1, g * BLOCKS), (g + 1) * BLOCKS, send, 0)

    def combine(g):
        span = pl.ds(g * BLOCKS, BLOCKS)
        received(returned.at[span], ret_sem.at[g])
        block = returned[span].reshape(ROWS, OWN)
        number = (lax.broadcasted_iota(jnp.int32, (256, 128), 1) + g * ROWS).astype(F32)

        def add(b, carry):
            at = pl.ds(pl.multiple_of(b * 256, 256), 256)
            place = place_col[at, :]
            chosen = jnp.concatenate(
                [(place == number).astype(F32), (place == number + 128.0).astype(F32)], axis=1
            ).astype(BF16)
            total[at, :] += jnp.dot(chosen, block, preferred_element_type=F32)
            return carry

        lax.fori_loop(0, TOKENS // 256, add, 0)

    dispatch(0)
    dispatch(1)
    for load in loads:
        load.wait()

    def step(s, carry):
        pl.when(s < GROUPS)(lambda: gather(s))
        pl.when(s + 2 < GROUPS)(lambda: dispatch(s + 2))
        pl.when((s >= 1) & (s < GROUPS + 1))(lambda: forward(s - 1))
        pl.when((s >= 2) & (s < GROUPS + 2))(lambda: expert(s - 2))
        pl.when((s >= 3) & (s < GROUPS + 3))(lambda: relay(s - 3))
        pl.when((s >= 4) & (s < GROUPS + 4))(lambda: give_back(s - 4))
        pl.when(s >= 5)(lambda: combine(s - 5))
        return carry

    lax.fori_loop(0, GROUPS + 5, step, 0)
    out[...] = (conv[...].astype(F32) + total[...]).astype(BF16)

    most, half = pl.ds(0, EXPERTS - 1), pl.ds(0, EXPERTS // 2)
    sent(rim_out.at[most], send_sem.at[0])
    sent(pick_out.at[most], send_sem.at[1])
    sent(outgoing.at[most], send_sem.at[2])
    sent(outgoing, send_sem.at[3])
    sent(outgoing, send_sem.at[4])
    sent(outgoing.at[half], send_sem.at[5])
    sent(outgoing.at[half], send_sem.at[6])
    sent(outgoing.at[half], send_sem.at[7])
    sent(outgoing.at[half], send_sem.at[8])
    sent(outgoing, send_sem.at[9])
    sent(outgoing, send_sem.at[10])
    sent(final.at[most], send_sem.at[11])


def shards(
    pixels,
    conv_weight,
    norm_gain,
    router_weight,
    gate_weight,
    up_weight,
    down_weight,
    expert_ids,
    neighbours,
):
    vmem = pl.BlockSpec(memory_space=pltpu.VMEM)
    hbm = pl.BlockSpec(memory_space=pltpu.HBM)
    blocks = (EXPERTS, CAP, OWN)
    per_group = pltpu.SemaphoreType.DMA((GROUPS,))
    return pl.pallas_call(
        kernel,
        out_shape=jax.ShapeDtypeStruct((TOKENS, OWN), BF16),
        in_specs=[vmem] * 6 + [hbm] * 3,
        out_specs=vmem,
        scratch_shapes=[
            pltpu.VMEM((SIDE + 2, SIDE + 2 * LEFT, OWN), F32),
            pltpu.VMEM((EXPERTS, 8, 128), F32),
            pltpu.VMEM((EXPERTS, 8, 128), F32),
            pltpu.VMEM((EXPERTS, 8, 128), F32),
            pltpu.VMEM((EXPERTS, 8, 128), F32),
            pltpu.VMEM((TOKENS, OWN), BF16),
            pltpu.VMEM((1, TOKENS), F32),
            pltpu.VMEM((TOKENS, 128), F32),
            pltpu.VMEM((WIDTH, 128), BF16),
            pltpu.VMEM((WIDTH, UNITS), BF16),
            pltpu.VMEM((WIDTH, UNITS), BF16),
            pltpu.VMEM((UNITS, WIDTH), BF16),
            pltpu.VMEM(blocks, BF16),
            pltpu.VMEM((PARTS,) + blocks, BF16),
            pltpu.VMEM((ROWS, WIDTH), BF16),
            pltpu.VMEM((ROWS, UNITS), BF16),
            pltpu.VMEM((PARTS,) + blocks, BF16),
            pltpu.VMEM((EXPERTS // 2, CAP, OWN), BF16),
            pltpu.VMEM((EXPERTS // 2, CAP, OWN), BF16),
            pltpu.VMEM(blocks, BF16),
            pltpu.VMEM(blocks, BF16),
            pltpu.VMEM(blocks, BF16),
            pltpu.VMEM(blocks, BF16),
            pltpu.VMEM((TOKENS, OWN), F32),
            pltpu.SemaphoreType.DMA((3,)),
            pltpu.SemaphoreType.DMA((12,)),
            pltpu.SemaphoreType.DMA((2,)),
        ]
        + [per_group] * 10,
        compiler_params=pltpu.CompilerParams(
            collective_id=0, has_side_effects=True, vmem_limit_bytes=48 * 1024 * 1024
        ),
    )(
        pixels,
        conv_weight,
        norm_gain.reshape(PARTS, OWN),
        router_weight.reshape(1, WIDTH),
        expert_ids.reshape(1, TOKENS),
        neighbours,
        gate_weight,
        up_weight,
        down_weight,
    )


def solution(mesh):
    in_specs = (
        P("expert", "hidden"),
        P(None, "hidden"),
        P(),
        P(None, "expert"),
        P("expert", None, "hidden"),
        P("expert", None, "hidden"),
        P("expert", "hidden", None),
        P("expert", None),
        P("expert", None),
    )
    out_specs = P("expert", "hidden")
    return jax.shard_map(shards, mesh=mesh, in_specs=in_specs, out_specs=out_specs, check_vma=False)
```

time: 381 us -> 133 us (0.35)
  waiting for transfers between devices: 172 us -> 0 us
  Pallas kernels: 0 us -> 124 us
  blocking collectives: 108 us -> 0 us
  between operations: 27.8 us -> 0.02 us
  other arithmetic: 24.9 us -> 0 us
  matrix products: 23 us -> 0 us
  starting transfers between devices: 10.7 us -> 0 us
  local copies, waits for them, and re-layouts: 13.8 us -> 8.46 us
    pallas_call x0 -> x1, Pallas kernels: none -> 124 us  [shards(): pl.pallas_call(kernel, out_shape=jax.ShapeDtypeStruct((TOKENS, OWN), BF16...]
    all_to_all x1 -> x0, blocking collectives: 108 us -> none  [shards(): lax.all_to_all(buffer, 'expert', split_axis=0, concat_axis=0, tiled=True)]
    all_gather x2 -> x0, waiting for transfers between devices: 97.8 us -> none  [the longest x1 65.2 us: shards(): lax.all_gather(rim_cells, 'expert', axis=0, tiled=True)]
    reduce_scatter x1 -> x0, waiting for transfers between devices: 45.8 us -> none  [shards(): lax.psum_scatter(lax.dot_general(columns, hidden, (((0,), (1,)), ((), ())...]
    all_to_all x1 -> x0, waiting for transfers between devices: 28.5 us -> none  [shards(): lax.all_to_all(outgoing, 'expert', split_axis=0, concat_axis=0, tiled=True)]
    dot_general x4 -> x0, matrix products: 23 us -> none  [the longest x1 14.6 us: shards(): lax.dot_general(columns, hidden, (((0,), (1,)), ((), ())), preferred_elem...]
    all_to_all x1 -> x0, starting transfers between devices: 10.6 us -> none  [shards(): lax.all_to_all(outgoing, 'expert', split_axis=0, concat_axis=0, tiled=True)]
    scatter x1 -> x0, other arithmetic: 8.98 us -> none  [shards(): jnp.zeros((experts * capacity, whole.shape[1]), jnp.bfloat16).at[position]]
  transfers between devices with their start and end apart: 4 -> 0, of which waited for: 4 -> 0; matrix products, arithmetic and copies ran while one was open for 1% -> 0% of each run, Pallas kernels for 0% -> 0%
where the time goes in v1:
time: 133 us
  Pallas kernels  124 us (93%)
  local copies, waits for them, and re-layouts  8.46 us (6%)
    pallas_call x1, Pallas kernels, shards(): pl.pallas_call(kernel, out_shape=jax.ShapeDtypeStruct((TOKENS, OWN), BF16...  124 us
    unnamed x15, local copies, waits for them, and re-layouts  7.76 us

profile of v1, /device:TPU:1, one launch (start us, length us, event | category | flops | bytes accessed | tf_op | source)
XLA Modules:
  0.0 132.6 jit_solution(8713798590838820704)
XLA Ops:
  0.0 0.7 reshape.9.norm_gain
  0.7 0.0 copy-start
  0.7 1.6 %copy-done = bf16[1,1024,1024]{2,1,0:T(8,128)(2,1)S(1)} copy-done((bf16[1,1024,1024]{2,1,0:T(8,128)(2,1)S(1)}, bf16[1,1024,1024]{2,1,0:T(8,128)(2,1)}, u32[]{:S(2)}) %copy-start) | copy-done | bytes 2097176
  2.3 0.0 copy-start.1
  2.3 1.6 %copy-done.1 = bf16[1,1024,1024]{2,1,0:T(8,128)(2,1)S(1)} copy-done((bf16[1,1024,1024]{2,1,0:T(8,128)(2,1)S(1)}, bf16[1,1024,1024]{2,1,0:T(8,128)(2,1)}, u32[]{:S(2)}) %copy-start.1) | copy-done | bytes 2097176
  3.9 0.0 copy-start.2
  3.9 1.0 copy-done.2
  4.9 0.0 copy-start.3
  4.9 0.7 copy-done.3
  5.6 0.0 copy-start.4
  5.6 0.7 copy-done.4
  6.3 0.0 copy-start.5
  6.3 0.7 copy-done.5
  7.0 0.0 copy-start.6
  7.0 0.7 copy-done.6
  7.7 124.2 %shard_map.91 = bf16[1024,256]{1,0:T(8,128)(2,1)S(1)} custom-call(bf16[1024,256]{1,0:T(8,128)(2,1)S(1)} %copy-done.2, f32[9,256]{1,0:T(8,128)S(1)} %copy-done.3, f32[4,256]{1,0:T(4,128)S(1)} %reshape.9.norm_gain, bf16[1,1024]{1,0:T(2,128)(2,1)S(1)} %bitcast.2, s32[1,1024]{1,0:T(1,128)S(1)} %bitcast.3, s32[1,8]{1,0:T(1,128)S(1)} %copy-done.6, ...), custom_call_target="tpu_custom_call" | custom-call | tf_op jit(solution)/shard_map/pallas_call | solution.py:415
  131.8 0.8 copy.11
Async XLA Ops:
  0.7 1.6 %copy-start = (bf16[1,1024,1024]{2,1,0:T(8,128)(2,1)S(1)}, bf16[1,1024,1024]{2,1,0:T(8,128)(2,1)}, u32[]{:S(2)}) copy-start(bf16[1,1024,1024]{2,1,0:T(8,128)(2,1)} %gate_hbm.1) | copy-start | bytes 6291460
  2.3 1.6 %copy-start.1 = (bf16[1,1024,1024]{2,1,0:T(8,128)(2,1)S(1)}, bf16[1,1024,1024]{2,1,0:T(8,128)(2,1)}, u32[]{:S(2)}) copy-start(bf16[1,1024,1024]{2,1,0:T(8,128)(2,1)} %up_hbm.1) | copy-start | bytes 6291460
  3.9 1.0 copy-start.2
  4.9 0.7 copy-start.3
  5.6 0.7 copy-start.4
  6.3 0.7 copy-start.5
  7.0 0.7 copy-start.6

commit v2 on v1

v2 whole, which is shorter than its diff:
```python
import jax
import jax.numpy as jnp
from jax import lax
from jax.experimental import pallas as pl
from jax.experimental.pallas import tpu as pltpu
from jax.sharding import PartitionSpec as P

MESH = pl.DeviceIdType.MESH
F32 = jnp.float32
BF16 = jnp.bfloat16

SIDE = 32
TOKENS = SIDE * SIDE
EXPERTS = 64
CAP = 32
OWN = 256
PARTS = 4
UNITS = 1024
WIDTH = OWN * PARTS
GROUPS = 8
BLOCKS = EXPERTS // GROUPS
HALF = BLOCKS // 2
ROWS = BLOCKS * CAP
CHIPS = EXPERTS // 2
EDGE = 4 * SIDE
INNER = TOKENS - 2 * SIDE
OWN_BLOCK = 24
LEFT = 8
EPSILON = 1e-05


def kernel(
    pixels,
    conv_weight,
    norm_gain,
    router,
    ids,
    table,
    gate_hbm,
    up_hbm,
    down_hbm,
    out,
    pixels_in,
    taps,
    gain_in,
    router_in,
    ids_in,
    table_in,
    padded,
    rim_wide,
    rim_out,
    rim_in,
    held,
    pick_wide,
    pick_out,
    pick_in,
    conv,
    parts_row,
    place_row,
    place_col,
    router_wide,
    gate_w,
    up_w,
    down_w,
    outgoing,
    rows,
    normed,
    hidden,
    partial,
    relay_dn,
    relay_up,
    sums_dn,
    sums_up,
    final,
    returned,
    total,
    load_sem,
    send_sem,
    rim_sem,
    src_sem,
    disp_sem,
    gat_dn,
    gat_up,
    fwd_dn,
    fwd_up,
    rel_dn,
    rel_up,
    sum_dn,
    sum_up,
    ret_sem,
):
    e = lax.axis_index("expert")
    y = lax.axis_index("hidden")
    x, z, c = lax.div(e, 16), lax.rem(lax.div(e, 2), 8), lax.rem(e, 2)
    chip = lax.div(e, 2)
    up, dn, op = lax.rem(y + 1, 4), lax.rem(y + 3, 4), lax.rem(y + 2, 4)

    def is_near(g):
        return (g == 3) | (g == 5) | (g == 7)

    def offsets(k):
        g, i = lax.div(k, BLOCKS), lax.rem(k, BLOCKS)
        turn = jnp.where(
            is_near(g), lax.div(g + 5, 2) - 4, jnp.where(g < 3, g, jnp.where(g == 4, 3, 4))
        )
        third = lax.rem(i + turn, 3)
        dz = jnp.where(is_near(g), jnp.where(third == 2, 7, third), 2 + lax.rem(i + turn, 5))
        return lax.div(i, 2), lax.rem(i, 2), dz

    def ahead(k):
        dx, dc, dz = offsets(k)
        return (lax.rem(x + dx, 4) * 8 + lax.rem(z + dz, 8)) * 2 + lax.rem(c + dc, 2)

    def behind(k):
        dx, dc, dz = offsets(k)
        return (lax.rem(x + 4 - dx, 4) * 8 + lax.rem(z + 8 - dz, 8)) * 2 + lax.rem(c + dc, 2)

    def chip_ahead(k):
        return lax.rem(x + lax.div(k, 8), 4) * 8 + lax.rem(z + lax.rem(k, 8), 8)

    def remote(src, dst, sent, got, target):
        return pltpu.make_async_remote_copy(
            src_ref=src,
            dst_ref=dst,
            send_sem=sent,
            recv_sem=got,
            device_id=target,
            device_id_type=MESH,
        )

    def received(dst, sem):
        remote(dst, dst, send_sem.at[0], sem, (e, up)).wait_recv()

    def sent(src, sem):
        remote(src, src, sem, rim_sem.at[0], (e, up)).wait_send()

    loads = [
        pltpu.make_async_copy(source, target, load_sem.at[i])
        for i, (source, target) in enumerate(
            (
                (pixels, pixels_in),
                (table, table_in),
                (ids, ids_in),
                (router, router_in),
                (conv_weight, taps),
                (norm_gain, gain_in),
                (gate_hbm.at[0], gate_w),
                (up_hbm.at[0], up_w),
                (down_hbm.at[0], down_w),
            )
        )
    ]
    for load in loads:
        load.start()

    barrier = pltpu.get_barrier_semaphore()

    def greet(k, carry):
        target = lax.rem(e + k, EXPERTS)
        pl.semaphore_signal(barrier, inc=1, device_id=(target, y), device_id_type=MESH)
        return carry

    lax.fori_loop(1, EXPERTS, greet, 0)
    pl.semaphore_signal(barrier, inc=1, device_id=(e, up), device_id_type=MESH)
    pl.semaphore_signal(barrier, inc=1, device_id=(e, dn), device_id_type=MESH)

    padded[...] = jnp.zeros_like(padded)
    rim_wide[...] = jnp.zeros_like(rim_wide)
    conv[:, 0:SIDE] = jnp.zeros((PARTS, SIDE, OWN), BF16)
    conv[:, TOKENS - SIDE : TOKENS] = jnp.zeros((PARTS, SIDE, OWN), BF16)
    for load in loads[:6]:
        load.wait()

    def widen(i, carry):
        at = pl.multiple_of(i * SIDE, SIDE)
        padded[i + 1, LEFT : LEFT + SIDE, :] = pixels_in[pl.ds(at, SIDE), :].astype(F32)
        return carry

    lax.fori_loop(0, SIDE, widen, 0)
    near, far = LEFT, LEFT + SIDE - 1
    for half in range(2):
        lanes = slice(128 * half, 128 * half + 128)
        rim_wide[:, half, :] = padded[1, near : far + 1, lanes]
        rim_wide[:, 2 + half, :] = padded[SIDE, near : far + 1, lanes]
        rim_wide[:, 4 + half, :] = padded[1 : SIDE + 1, near, lanes]
        rim_wide[:, 6 + half, :] = padded[1 : SIDE + 1, far, lanes]
    rim_wide[:, 8, 0:8] = jnp.broadcast_to(table_in[...].astype(F32), (CHIPS, 8))
    rim_out[...] = rim_wide[...].astype(BF16)
    rim_in[c, chip] = rim_out[chip]

    def convolve(i, carry):
        mixed = padded[i + 1, near : far + 1, :]
        for a in range(3):
            for b in range(3):
                tap = taps[3 * a + b : 3 * a + b + 1, :]
                mixed = mixed + tap * padded[i + a, near - 1 + b : far + b, :]
        rounded = mixed.astype(BF16)
        conv[y, pl.ds(pl.multiple_of(i * SIDE, SIDE), SIDE), :] = rounded
        total[i] = rounded.astype(F32)
        return carry

    lax.fori_loop(0, SIDE, convolve, 0)

    pl.semaphore_wait(barrier, EXPERTS - 1 + 2)

    def send_rim(k, carry):
        target = chip_ahead(k)
        remote(
            rim_out.at[target],
            rim_in.at[c, chip],
            send_sem.at[0],
            rim_sem.at[0],
            (target * 2 + c, y),
        ).start()
        return carry

    lax.fori_loop(1, CHIPS, send_rim, 0)

    first_half, second_half = pl.ds(SIDE, INNER // 2), pl.ds(SIDE + INNER // 2, INNER // 2)
    remote(
        conv.at[y, first_half], conv.at[y, first_half], send_sem.at[12], src_sem.at[0], (e, up)
    ).start()
    remote(
        conv.at[y, second_half], conv.at[y, second_half], send_sem.at[12], src_sem.at[1], (e, dn)
    ).start()
    remote(
        conv.at[y, second_half], conv.at[y, second_half], send_sem.at[12], src_sem.at[2], (e, up)
    ).start()
    remote(
        conv.at[y, first_half], conv.at[y, first_half], send_sem.at[12], src_sem.at[3], (e, dn)
    ).start()

    onehot = (
        ids_in[...] == lax.broadcasted_iota(jnp.int32, (EXPERTS, TOKENS), 0)
    ).astype(F32)
    onehot_bf = onehot.astype(BF16)
    parts_row[...] = jnp.zeros_like(parts_row)

    def places(b, carry):
        at = pl.multiple_of(b * 256, 256)
        earlier = lax.broadcasted_iota(jnp.int32, (TOKENS, 256), 0) < (
            lax.broadcasted_iota(jnp.int32, (TOKENS, 256), 1) + at
        )
        counts = jnp.dot(
            onehot_bf, earlier.astype(F32).astype(BF16), preferred_element_type=F32
        )
        own = ids_in[0:1, pl.ds(at, 256)]
        chosen = own == lax.broadcasted_iota(jnp.int32, (EXPERTS, 256), 0)
        slot = jnp.sum(jnp.where(chosen, counts, 0.0), axis=0, keepdims=True)
        dx = (lax.shift_right_logical(own, 4) - x + 4) & 3
        dz = ((lax.shift_right_logical(own, 1) & 7) - z + 8) & 7
        dc = ((own & 1) + c) & 1
        i = dx * 2 + dc
        third = jnp.where(dz == 7, 2, dz) + 9 - i
        third = jnp.where(third >= 6, third - 6, third)
        third = jnp.where(third >= 3, third - 3, third)
        fifth = dz + 8 - i
        fifth = jnp.where(fifth >= 10, fifth - 10, jnp.where(fifth >= 5, fifth - 5, fifth))
        is_close = (dz <= 1) | (dz == 7)
        group = jnp.where(
            is_close, 3 + 2 * third, jnp.where(fifth < 3, fifth, 2 * fifth - 2)
        )
        block = (group * BLOCKS + i).astype(F32)
        place = block * CAP + slot
        number = lax.broadcasted_iota(jnp.int32, (1, 256), 1) + at
        row, column = lax.shift_right_logical(number, 5), number & 31
        inner = (row >= 1) & (row <= SIDE - 2) & (column >= 1) & (column <= SIDE - 2)
        place_row[0:1, pl.ds(at, 256)] = jnp.where(inner, place, -1.0)
        parts_row[0:1, pl.ds(at, 256)] = block
        parts_row[1:2, pl.ds(at, 256)] = slot
        place_col[pl.ds(at, 256), :] = jnp.broadcast_to(place, (128, 256)).T
        return carry

    lax.fori_loop(0, TOKENS // 256, places, 0)

    number = lax.broadcasted_iota(jnp.int32, (1, EDGE), 1)
    along = number & 31
    edge = lax.shift_right_logical(number, 5)
    pixel = jnp.where(
        edge == 0,
        along,
        jnp.where(
            edge == 1,
            along + (TOKENS - SIDE),
            jnp.where(edge == 2, along * SIDE, along * SIDE + SIDE - 1),
        ),
    )
    picks = (lax.broadcasted_iota(jnp.int32, (TOKENS, EDGE), 0) == pixel).astype(F32).astype(BF16)
    border = jnp.dot(parts_row[...].astype(BF16), picks, preferred_element_type=F32)
    counted = (edge <= 1) | ((along >= 1) & (along <= SIDE - 2))
    place_row[0:1, TOKENS : TOKENS + EDGE] = jnp.where(
        counted, border[0:1] * CAP + border[1:2], -1.0
    )

    def widen_router(b, carry):
        at = pl.multiple_of(b * 256, 256)
        column = router_in[0:1, pl.ds(at, 256)].astype(F32)
        router_wide[pl.ds(at, 256), :] = jnp.broadcast_to(column, (128, 256)).T.astype(BF16)
        return carry

    received(rim_in.at[c, pl.ds(0, CHIPS - 1)], rim_sem.at[0])
    other = e + 1 - 2 * c
    remote(rim_in.at[c], rim_in.at[c], send_sem.at[13], rim_sem.at[2], (other, y)).start()
    held[c] = rim_in[c].astype(F32)
    received(rim_in.at[1 - c], rim_sem.at[2])
    held[1 - c] = rim_in[1 - c].astype(F32)
    tables = held[c, :, 8, :]
    tile = lax.broadcasted_iota(jnp.int32, (CHIPS, EXPERTS), 1)
    tile = ((tile & 31) * 2 + lax.shift_right_logical(tile, 5)).astype(F32)
    edges = [
        jnp.concatenate(
            [
                jnp.concatenate([held[core, :, 2 * side + half, :] for half in range(2)], axis=1)
                for core in range(2)
            ],
            axis=0,
        ).astype(BF16)
        for side in range(4)
    ]
    for direction, side in enumerate((1, 0, 3, 2, 1, 1, 0, 0)):
        chosen = (tables[:, direction : direction + 1] == tile).astype(F32).astype(BF16)
        found = jnp.dot(chosen, edges[side], preferred_element_type=F32)
        pick_wide[:, 2 * direction, :] = found[:, 0:128]
        pick_wide[:, 2 * direction + 1, :] = found[:, 128:256]
    pick_out[...] = pick_wide[...].astype(BF16)

    def send_pick(k, carry):
        target = chip_ahead(k)
        remote(
            pick_out.at[target],
            pick_in.at[chip],
            send_sem.at[1],
            rim_sem.at[1],
            (target * 2 + c, y),
        ).start()
        return carry

    lax.fori_loop(1, CHIPS, send_pick, 0)
    pick_in[chip] = pick_out[chip]

    lax.fori_loop(0, WIDTH // 256, widen_router, 0)
    received(conv.at[dn, first_half], src_sem.at[0])
    remote(
        conv.at[dn, first_half], conv.at[dn, first_half], send_sem.at[14], src_sem.at[4], (e, up)
    ).start()
    received(conv.at[up, second_half], src_sem.at[1])
    remote(
        conv.at[up, second_half], conv.at[up, second_half], send_sem.at[14], src_sem.at[5], (e, dn)
    ).start()

    received(pick_in.at[pl.ds(0, CHIPS - 1)], rim_sem.at[1])
    pick_wide[...] = pick_in[...].astype(F32)
    for half in range(2):
        lanes = slice(128 * half, 128 * half + 128)
        padded[0, near : far + 1, lanes] = pick_wide[:, half, :]
        padded[SIDE + 1, near : far + 1, lanes] = pick_wide[:, 2 + half, :]
        padded[1 : SIDE + 1, near - 1, lanes] = pick_wide[:, 4 + half, :]
        padded[1 : SIDE + 1, far + 1, lanes] = pick_wide[:, 6 + half, :]
        last = SIDE - 1
        padded[0, near - 1 : near, lanes] = pick_wide[last, 8 + half : 9 + half, :]
        padded[0, far + 1 : far + 2, lanes] = pick_wide[0, 10 + half : 11 + half, :]
        padded[SIDE + 1, near - 1 : near, lanes] = pick_wide[last, 12 + half : 13 + half, :]
        padded[SIDE + 1, far + 1 : far + 2, lanes] = pick_wide[0, 14 + half : 15 + half, :]

    def mix(center, window):
        mixed = center
        for a in range(3):
            for b in range(3):
                mixed = mixed + taps[3 * a + b : 3 * a + b + 1, :] * window(a, b)
        return mixed.astype(BF16)

    left = mix(
        padded[1 : SIDE + 1, near, :], lambda a, b: padded[a : a + SIDE, near - 1 + b, :]
    )
    right = mix(padded[1 : SIDE + 1, far, :], lambda a, b: padded[a : a + SIDE, far - 1 + b, :])
    top = mix(padded[1, near : far + 1, :], lambda a, b: padded[a, near - 1 + b : far + b, :])
    bottom = mix(
        padded[SIDE, near : far + 1, :],
        lambda a, b: padded[SIDE - 1 + a, near - 1 + b : far + b, :],
    )
    for i, strip in enumerate((top, bottom, left, right)):
        conv[y, TOKENS + i * SIDE : TOKENS + (i + 1) * SIDE, :] = strip
    total[:, 0, :] = left.astype(F32)
    total[:, SIDE - 1, :] = right.astype(F32)
    total[0] = top.astype(F32)
    total[SIDE - 1] = bottom.astype(F32)

    def blocks_of(g):
        first = lax.broadcasted_iota(jnp.int32, (ROWS, TOKENS + EDGE), 0) + g * ROWS
        return (place_row[...] == first.astype(F32)).astype(F32).astype(BF16)

    def dispatch_far(g):
        block = jnp.dot(blocks_of(g), conv[y], preferred_element_type=F32).astype(BF16)
        outgoing[y, pl.ds(g * BLOCKS, BLOCKS)] = block.reshape(BLOCKS, CAP, OWN)

        def send(k, carry):
            remote(
                outgoing.at[y, k], rows.at[y, k], send_sem.at[2], disp_sem.at[g], (ahead(k), y)
            ).start()
            return carry

        lax.fori_loop(g * BLOCKS, (g + 1) * BLOCKS, send, 0)

    def dispatch_near(g):
        chosen = blocks_of(g)
        for part in range(PARTS):
            block = jnp.dot(chosen, conv[part], preferred_element_type=F32).astype(BF16)
            outgoing[part, pl.ds(g * BLOCKS, BLOCKS)] = block.reshape(BLOCKS, CAP, OWN)

        @pl.when(g == 3)
        def _():
            pltpu.make_async_copy(
                outgoing.at[:, OWN_BLOCK], rows.at[:, OWN_BLOCK], disp_sem.at[3]
            ).start()

        def send(k, carry):
            remote(
                outgoing.at[:, k], rows.at[:, k], send_sem.at[15], disp_sem.at[g], (ahead(k), y)
            ).start()
            return carry

        lax.fori_loop(g * BLOCKS + jnp.where(g == 3, 1, 0), (g + 1) * BLOCKS, send, 0)

    pack = pl.ds(TOKENS, EDGE)
    pack_low, pack_high = pl.ds(TOKENS, EDGE // 2), pl.ds(TOKENS + EDGE // 2, EDGE // 2)

    def forward_pack():
        received(conv.at[dn, pack], src_sem.at[6])
        remote(
            conv.at[dn, pack_low], conv.at[dn, pack_low], send_sem.at[17], src_sem.at[8], (e, up)
        ).start()
        received(conv.at[up, pack], src_sem.at[7])
        remote(
            conv.at[up, pack_high], conv.at[up, pack_high], send_sem.at[17], src_sem.at[9], (e, dn)
        ).start()

    def conv_complete():
        received(conv.at[dn, second_half], src_sem.at[2])
        received(conv.at[up, first_half], src_sem.at[3])
        received(conv.at[op, first_half], src_sem.at[4])
        received(conv.at[op, second_half], src_sem.at[5])
        received(conv.at[op, pack_low], src_sem.at[8])
        received(conv.at[op, pack_high], src_sem.at[9])

    def gather(g):
        span = pl.ds(g * BLOCKS, BLOCKS)
        mine = rows.at[y, span]
        received(mine, disp_sem.at[g])
        remote(mine, mine, send_sem.at[3], gat_dn.at[g], (e, up)).start()
        remote(mine, mine, send_sem.at[4], gat_up.at[g], (e, dn)).start()

    def forward(g):
        received(rows.at[dn, pl.ds(g * BLOCKS, BLOCKS)], gat_dn.at[g])
        low = rows.at[dn, pl.ds(g * BLOCKS, HALF)]
        remote(low, low, send_sem.at[5], fwd_dn.at[g], (e, up)).start()
        received(rows.at[up, pl.ds(g * BLOCKS, BLOCKS)], gat_up.at[g])
        high = rows.at[up, pl.ds(g * BLOCKS + HALF, HALF)]
        remote(high, high, send_sem.at[6], fwd_up.at[g], (e, dn)).start()

    def arrived(g):
        received(rows.at[op, pl.ds(g * BLOCKS, HALF)], fwd_dn.at[g])
        received(rows.at[op, pl.ds(g * BLOCKS + HALF, HALF)], fwd_up.at[g])

    def expert(g):
        span = pl.ds(g * BLOCKS, BLOCKS)
        pl.when(is_near(g))(lambda: received(rows.at[:, span], disp_sem.at[g]))
        pl.when(jnp.logical_not(is_near(g)))(lambda: arrived(g))
        squares = jnp.zeros((ROWS, 1), F32)
        for part in range(PARTS):
            wide = rows[part, span].reshape(ROWS, OWN).astype(F32)
            squares = squares + jnp.sum(wide * wide, axis=1, keepdims=True)
        scale = lax.rsqrt(squares * (1.0 / WIDTH) + EPSILON)
        for part in range(PARTS):
            wide = rows[part, span].reshape(ROWS, OWN).astype(F32)
            normed[:, part * OWN : (part + 1) * OWN] = (
                wide * scale * gain_in[0:1, part * OWN : (part + 1) * OWN]
            ).astype(BF16)
        score = jnp.dot(normed[...], router_wide[...], preferred_element_type=F32)
        weight = 1.0 / (1.0 + jnp.exp(-score))
        weight = jnp.concatenate([weight, weight], axis=1)

        def units(n, carry):
            at = pl.ds(pl.multiple_of(n * 256, 256), 256)
            gate = jnp.dot(normed[...], gate_w[:, at], preferred_element_type=F32)
            lift = jnp.dot(normed[...], up_w[:, at], preferred_element_type=F32)
            hidden[:, at] = (gate / (1.0 + jnp.exp(-gate)) * lift * weight).astype(BF16)
            return carry

        lax.fori_loop(0, UNITS // 256, units, 0)

        def channels(part, carry):
            at = pl.ds(pl.multiple_of(part * OWN, OWN), OWN)
            result = jnp.dot(hidden[...], down_w[:, at], preferred_element_type=F32)
            partial[part, span] = result.astype(BF16).reshape(BLOCKS, CAP, OWN)
            return carry

        lax.fori_loop(0, PARTS, channels, 0)

        low, high = pl.ds(g * BLOCKS, HALF), pl.ds(g * BLOCKS + HALF, HALF)
        slot = pl.ds(g * HALF, HALF)
        remote(
            partial.at[op, low], relay_dn.at[slot], send_sem.at[7], rel_dn.at[g], (e, up)
        ).start()
        remote(
            partial.at[op, high], relay_up.at[slot], send_sem.at[8], rel_up.at[g], (e, dn)
        ).start()
        remote(
            partial.at[up, high], sums_dn.at[high], send_sem.at[9], sum_dn.at[g], (e, up)
        ).start()
        remote(
            partial.at[dn, low], sums_up.at[low], send_sem.at[10], sum_up.at[g], (e, dn)
        ).start()

    def relay(g):
        low, high = pl.ds(g * BLOCKS, HALF), pl.ds(g * BLOCKS + HALF, HALF)
        slot = pl.ds(g * HALF, HALF)
        received(relay_dn.at[slot], rel_dn.at[g])
        partial[up, low] = (partial[up, low].astype(F32) + relay_dn[slot].astype(F32)).astype(BF16)
        remote(
            partial.at[up, low], sums_dn.at[low], send_sem.at[9], sum_dn.at[g], (e, up)
        ).start()
        received(relay_up.at[slot], rel_up.at[g])
        partial[dn, high] = (
            partial[dn, high].astype(F32) + relay_up[slot].astype(F32)
        ).astype(BF16)
        remote(
            partial.at[dn, high], sums_up.at[high], send_sem.at[10], sum_up.at[g], (e, dn)
        ).start()

    def give_back(g):
        span = pl.ds(g * BLOCKS, BLOCKS)
        received(sums_dn.at[span], sum_dn.at[g])
        received(sums_up.at[span], sum_up.at[g])
        final[span] = (
            partial[y, span].astype(F32) + sums_dn[span].astype(F32) + sums_up[span].astype(F32)
        ).astype(BF16)

        @pl.when(g == 3)
        def _():
            pltpu.make_async_copy(
                final.at[OWN_BLOCK], returned.at[OWN_BLOCK], ret_sem.at[3]
            ).start()

        def send(k, carry):
            remote(
                final.at[k], returned.at[k], send_sem.at[11], ret_sem.at[g], (behind(k), y)
            ).start()
            return carry

        lax.fori_loop(g * BLOCKS + jnp.where(g == 3, 1, 0), (g + 1) * BLOCKS, send, 0)

    def combine(g):
        span = pl.ds(g * BLOCKS, BLOCKS)
        received(returned.at[span], ret_sem.at[g])
        block = returned[span].reshape(ROWS, OWN)
        number = (lax.broadcasted_iota(jnp.int32, (256, 128), 1) + g * ROWS).astype(F32)

        def add(b, carry):
            at = pl.ds(pl.multiple_of(b * 256, 256), 256)
            place = place_col[at, :]
            chosen = jnp.concatenate(
                [(place == number).astype(F32), (place == number + 128.0).astype(F32)], axis=1
            ).astype(BF16)
            tile_rows = pl.ds(b * 8, 8)
            added = jnp.dot(chosen, block, preferred_element_type=F32)
            total[tile_rows] += added.reshape(8, SIDE, OWN)
            return carry

        lax.fori_loop(0, TOKENS // 256, add, 0)

    dispatch_far(0)
    remote(conv.at[y, pack], conv.at[y, pack], send_sem.at[16], src_sem.at[6], (e, up)).start()
    remote(conv.at[y, pack], conv.at[y, pack], send_sem.at[16], src_sem.at[7], (e, dn)).start()
    dispatch_far(1)
    for load in loads[6:]:
        load.wait()

    def step(s, carry):
        pl.when((s < GROUPS) & jnp.logical_not(is_near(s)))(lambda: gather(s))
        pl.when(s == 0)(forward_pack)
        pl.when(s == 1)(conv_complete)
        pl.when((s + 2 < GROUPS) & is_near(s + 2))(lambda: dispatch_near(s + 2))
        pl.when((s + 2 < GROUPS) & jnp.logical_not(is_near(s + 2)))(lambda: dispatch_far(s + 2))
        pl.when((s >= 1) & (s < GROUPS + 1) & jnp.logical_not(is_near(s - 1)))(
            lambda: forward(s - 1)
        )
        pl.when((s >= 2) & (s < GROUPS + 2))(lambda: expert(s - 2))
        pl.when((s >= 3) & (s < GROUPS + 3))(lambda: relay(s - 3))
        pl.when((s >= 4) & (s < GROUPS + 4))(lambda: give_back(s - 4))
        pl.when(s >= 5)(lambda: combine(s - 5))
        return carry

    lax.fori_loop(0, GROUPS + 5, step, 0)
    out[...] = total[...].reshape(TOKENS, OWN).astype(BF16)

    def span_of(count):
        return outgoing.at[0, pl.ds(0, count)]

    sent(rim_out.at[pl.ds(0, CHIPS - 1)], send_sem.at[0])
    sent(pick_out.at[pl.ds(0, CHIPS - 1)], send_sem.at[1])
    sent(rim_in.at[0], send_sem.at[13])
    sent(span_of(40), send_sem.at[2])
    sent(span_of(40), send_sem.at[3])
    sent(span_of(40), send_sem.at[4])
    sent(span_of(20), send_sem.at[5])
    sent(span_of(20), send_sem.at[6])
    sent(span_of(32), send_sem.at[7])
    sent(span_of(32), send_sem.at[8])
    sent(span_of(64), send_sem.at[9])
    sent(span_of(64), send_sem.at[10])
    sent(span_of(63), send_sem.at[11])
    sent(conv.at[pl.ds(0, 2), pl.ds(0, INNER)], send_sem.at[12])
    sent(conv.at[0, pl.ds(0, INNER)], send_sem.at[14])
    sent(outgoing.at[:, pl.ds(0, 23)], send_sem.at[15])
    sent(conv.at[0, pl.ds(0, 2 * EDGE)], send_sem.at[16])
    sent(conv.at[0, pl.ds(0, EDGE)], send_sem.at[17])


def shards(
    pixels,
    conv_weight,
    norm_gain,
    router_weight,
    gate_weight,
    up_weight,
    down_weight,
    expert_ids,
    neighbours,
):
    vmem = pl.BlockSpec(memory_space=pltpu.VMEM)
    hbm = pl.BlockSpec(memory_space=pltpu.HBM)
    blocks = (EXPERTS, CAP, OWN)
    per_group = pltpu.SemaphoreType.DMA((GROUPS,))
    return pl.pallas_call(
        kernel,
        out_shape=jax.ShapeDtypeStruct((TOKENS, OWN), BF16),
        in_specs=[hbm] * 9,
        out_specs=vmem,
        scratch_shapes=[
            pltpu.VMEM((TOKENS, OWN), BF16),
            pltpu.VMEM((9, OWN), F32),
            pltpu.VMEM((1, WIDTH), F32),
            pltpu.VMEM((1, WIDTH), BF16),
            pltpu.VMEM((1, TOKENS), jnp.int32),
            pltpu.VMEM((1, 8), jnp.int32),
            pltpu.VMEM((SIDE + 2, SIDE + 2 * LEFT, OWN), F32),
            pltpu.VMEM((CHIPS, 16, 128), F32),
            pltpu.VMEM((CHIPS, 16, 128), BF16),
            pltpu.VMEM((2, CHIPS, 16, 128), BF16),
            pltpu.VMEM((2, CHIPS, 16, 128), F32),
            pltpu.VMEM((CHIPS, 16, 128), F32),
            pltpu.VMEM((CHIPS, 16, 128), BF16),
            pltpu.VMEM((CHIPS, 16, 128), BF16),
            pltpu.VMEM((PARTS, TOKENS + EDGE, OWN), BF16),
            pltpu.VMEM((8, TOKENS), F32),
            pltpu.VMEM((1, TOKENS + EDGE), F32),
            pltpu.VMEM((TOKENS, 128), F32),
            pltpu.VMEM((WIDTH, 128), BF16),
            pltpu.VMEM((WIDTH, UNITS), BF16),
            pltpu.VMEM((WIDTH, UNITS), BF16),
            pltpu.VMEM((UNITS, WIDTH), BF16),
            pltpu.VMEM((PARTS,) + blocks, BF16),
            pltpu.VMEM((PARTS,) + blocks, BF16),
            pltpu.VMEM((ROWS, WIDTH), BF16),
            pltpu.VMEM((ROWS, UNITS), BF16),
            pltpu.VMEM((PARTS,) + blocks, BF16),
            pltpu.VMEM((EXPERTS // 2, CAP, OWN), BF16),
            pltpu.VMEM((EXPERTS // 2, CAP, OWN), BF16),
            pltpu.VMEM(blocks, BF16),
            pltpu.VMEM(blocks, BF16),
            pltpu.VMEM(blocks, BF16),
            pltpu.VMEM(blocks, BF16),
            pltpu.VMEM((SIDE, SIDE, OWN), F32),
            pltpu.SemaphoreType.DMA((9,)),
            pltpu.SemaphoreType.DMA((18,)),
            pltpu.SemaphoreType.DMA((3,)),
            pltpu.SemaphoreType.DMA((10,)),
        ]
        + [per_group] * 10,
        compiler_params=pltpu.CompilerParams(
            collective_id=0, has_side_effects=True, vmem_limit_bytes=63 * 1024 * 1024
        ),
    )(
        pixels,
        conv_weight,
        norm_gain.reshape(1, WIDTH),
        router_weight.reshape(1, WIDTH),
        expert_ids.reshape(1, TOKENS),
        neighbours,
        gate_weight,
        up_weight,
        down_weight,
    )


def solution(mesh):
    in_specs = (
        P("expert", "hidden"),
        P(None, "hidden"),
        P(),
        P(None, "expert"),
        P("expert", None, "hidden"),
        P("expert", None, "hidden"),
        P("expert", "hidden", None),
        P("expert", None),
        P("expert", None),
    )
    out_specs = P("expert", "hidden")
    return jax.shard_map(shards, mesh=mesh, in_specs=in_specs, out_specs=out_specs, check_vma=False)
```

time: 133 us -> 116 us (0.87)
  Pallas kernels: 124 us -> 114 us
  local copies, waits for them, and re-layouts: 8.46 us -> 1.87 us
    pallas_call x1, Pallas kernels: 124 us -> 114 us  [shards(): pl.pallas_call(kernel, out_shape=jax.ShapeDtypeStruct((TOKENS, OWN), BF16...]
    unnamed x15 -> x1, local copies, waits for them, and re-layouts: 7.76 us -> 1.87 us
where the time goes in v2:
time: 116 us
  Pallas kernels  114 us (98%)
  local copies, waits for them, and re-layouts  1.87 us (2%)
    pallas_call x1, Pallas kernels, shards(): pl.pallas_call(kernel, out_shape=jax.ShapeDtypeStruct((TOKENS, OWN), BF16...  114 us

profile of v2, /device:TPU:1, one launch (start us, length us, event | category | flops | bytes accessed | tf_op | source)
XLA Modules:
  0.0 115.5 jit_solution(5731010980243551609)
XLA Ops:
  0.0 113.6 %shard_map.91 = bf16[1024,256]{1,0:T(8,128)(2,1)} custom-call(bf16[1024,256]{1,0:T(8,128)(2,1)} %pixels.1, f32[9,256]{1,0:T(8,128)} %conv_weight.1, f32[1,1024]{1,0:T(1,128)} %bitcast.3, bf16[1,1024]{1,0:T(2,128)(2,1)} %bitcast.4, s32[1,1024]{1,0:T(1,128)} %bitcast.5, s32[1,8]{1,0:T(1,128)} %table.1, bf16[1,1024,1024]{2,1,0:T(8,128)(2,1)} %gate_hbm.1, ...), custom_call_target="tpu_custom_call" | custom-call | tf_op jit(solution)/shard_map/pallas_call | solution.py:634
  113.7 1.9 %copy.11 = bf16[1024,256]{1,0:T(8,128)(2,1)} copy(bf16[1024,256]{1,0:T(8,128)(2,1)} %shard_map.91) | data formatting | bytes 1048576

commit v3 on v2

--- a/solution.py
+++ b/solution.py
@@ -100,12 +100,13 @@
 
     def offsets(k):
         g, i = lax.div(k, BLOCKS), lax.rem(k, BLOCKS)
-        turn = jnp.where(
-            is_near(g), lax.div(g + 5, 2) - 4, jnp.where(g < 3, g, jnp.where(g == 4, 3, 4))
-        )
-        third = lax.rem(i + turn, 3)
-        dz = jnp.where(is_near(g), jnp.where(third == 2, 7, third), 2 + lax.rem(i + turn, 5))
-        return lax.div(i, 2), lax.rem(i, 2), dz
+        dc = lax.rem(i, 2)
+        third = lax.rem(i + lax.div(g + 5, 2) + 2, 3)
+        hops = jnp.where((g == 0) | (g == 6), 2, jnp.where(g == 4, 4, 3))
+        flip = lax.rem(dc + jnp.where((g == 2) | (g == 6), 1, 0), 2)
+        far_dz = jnp.where(flip == 1, 8 - hops, hops)
+        dz = jnp.where(is_near(g), jnp.where(third == 2, 7, third), far_dz)
+        return lax.div(i, 2), dc, dz
 
     def ahead(k):
         dx, dc, dz = offsets(k)
@@ -254,12 +255,12 @@
         third = jnp.where(dz == 7, 2, dz) + 9 - i
         third = jnp.where(third >= 6, third - 6, third)
         third = jnp.where(third >= 3, third - 3, third)
-        fifth = dz + 8 - i
-        fifth = jnp.where(fifth >= 10, fifth - 10, jnp.where(fifth >= 5, fifth - 5, fifth))
         is_close = (dz <= 1) | (dz == 7)
-        group = jnp.where(
-            is_close, 3 + 2 * third, jnp.where(fifth < 3, fifth, 2 * fifth - 2)
+        flip = jnp.where(dz > 4, 1, 0) ^ dc
+        far_group = jnp.where(
+            dz == 4, 4, jnp.where((dz == 2) | (dz == 6), 6 * flip, 1 + flip)
         )
+        group = jnp.where(is_close, 3 + 2 * third, far_group)
         block = (group * BLOCKS + i).astype(F32)
         place = block * CAP + slot
         number = lax.broadcasted_iota(jnp.int32, (1, 256), 1) + at
@@ -449,17 +450,34 @@
         remote(mine, mine, send_sem.at[3], gat_dn.at[g], (e, up)).start()
         remote(mine, mine, send_sem.at[4], gat_up.at[g], (e, dn)).start()
 
+        @pl.when(g == 0)
+        def _():
+            remote(mine, mine, send_sem.at[18], fwd_dn.at[0], (e, op)).start()
+
     def forward(g):
         received(rows.at[dn, pl.ds(g * BLOCKS, BLOCKS)], gat_dn.at[g])
-        low = rows.at[dn, pl.ds(g * BLOCKS, HALF)]
-        remote(low, low, send_sem.at[5], fwd_dn.at[g], (e, up)).start()
+
+        @pl.when(g > 0)
+        def _():
+            low = rows.at[dn, pl.ds(g * BLOCKS, HALF)]
+            remote(low, low, send_sem.at[5], fwd_dn.at[g], (e, up)).start()
+
         received(rows.at[up, pl.ds(g * BLOCKS, BLOCKS)], gat_up.at[g])
-        high = rows.at[up, pl.ds(g * BLOCKS + HALF, HALF)]
-        remote(high, high, send_sem.at[6], fwd_up.at[g], (e, dn)).start()
+
+        @pl.when(g > 0)
+        def _():
+            high = rows.at[up, pl.ds(g * BLOCKS + HALF, HALF)]
+            remote(high, high, send_sem.at[6], fwd_up.at[g], (e, dn)).start()
 
     def arrived(g):
-        received(rows.at[op, pl.ds(g * BLOCKS, HALF)], fwd_dn.at[g])
-        received(rows.at[op, pl.ds(g * BLOCKS + HALF, HALF)], fwd_up.at[g])
+        @pl.when(g == 0)
+        def _():
+            received(rows.at[op, pl.ds(g * BLOCKS, BLOCKS)], fwd_dn.at[g])
+
+        @pl.when(g > 0)
+        def _():
+            received(rows.at[op, pl.ds(g * BLOCKS, HALF)], fwd_dn.at[g])
+            received(rows.at[op, pl.ds(g * BLOCKS + HALF, HALF)], fwd_up.at[g])
 
     def expert(g):
         span = pl.ds(g * BLOCKS, BLOCKS)
@@ -488,28 +506,29 @@
 
         lax.fori_loop(0, UNITS // 256, units, 0)
 
-        def channels(part, carry):
+        def channels(part):
             at = pl.ds(pl.multiple_of(part * OWN, OWN), OWN)
             result = jnp.dot(hidden[...], down_w[:, at], preferred_element_type=F32)
             partial[part, span] = result.astype(BF16).reshape(BLOCKS, CAP, OWN)
-            return carry
-
-        lax.fori_loop(0, PARTS, channels, 0)
 
         low, high = pl.ds(g * BLOCKS, HALF), pl.ds(g * BLOCKS + HALF, HALF)
         slot = pl.ds(g * HALF, HALF)
+        channels(op)
         remote(
             partial.at[op, low], relay_dn.at[slot], send_sem.at[7], rel_dn.at[g], (e, up)
         ).start()
         remote(
             partial.at[op, high], relay_up.at[slot], send_sem.at[8], rel_up.at[g], (e, dn)
         ).start()
+        channels(up)
         remote(
             partial.at[up, high], sums_dn.at[high], send_sem.at[9], sum_dn.at[g], (e, up)
         ).start()
+        channels(dn)
         remote(
             partial.at[dn, low], sums_up.at[low], send_sem.at[10], sum_up.at[g], (e, dn)
         ).start()
+        channels(y)
 
     def relay(g):
         low, high = pl.ds(g * BLOCKS, HALF), pl.ds(g * BLOCKS + HALF, HALF)
@@ -572,25 +591,28 @@
     remote(conv.at[y, pack], conv.at[y, pack], send_sem.at[16], src_sem.at[6], (e, up)).start()
     remote(conv.at[y, pack], conv.at[y, pack], send_sem.at[16], src_sem.at[7], (e, dn)).start()
     dispatch_far(1)
+    dispatch_far(2)
+    forward_pack()
     for load in loads[6:]:
         load.wait()
 
     def step(s, carry):
-        pl.when((s < GROUPS) & jnp.logical_not(is_near(s)))(lambda: gather(s))
-        pl.when(s == 0)(forward_pack)
-        pl.when(s == 1)(conv_complete)
-        pl.when((s + 2 < GROUPS) & is_near(s + 2))(lambda: dispatch_near(s + 2))
-        pl.when((s + 2 < GROUPS) & jnp.logical_not(is_near(s + 2)))(lambda: dispatch_far(s + 2))
+        pl.when((s < GROUPS) & jnp.logical_not(is_near(s)))(
+            lambda: gather(s)
+        )
         pl.when((s >= 1) & (s < GROUPS + 1) & jnp.logical_not(is_near(s - 1)))(
             lambda: forward(s - 1)
         )
+        pl.when(s == 0)(conv_complete)
         pl.when((s >= 2) & (s < GROUPS + 2))(lambda: expert(s - 2))
         pl.when((s >= 3) & (s < GROUPS + 3))(lambda: relay(s - 3))
+        pl.when((s >= 6) & (s < GROUPS + 6))(lambda: combine(s - 6))
         pl.when((s >= 4) & (s < GROUPS + 4))(lambda: give_back(s - 4))
-        pl.when(s >= 5)(lambda: combine(s - 5))
+        pl.when((s + 3 < GROUPS) & is_near(s + 3))(lambda: dispatch_near(s + 3))
+        pl.when((s + 3 < GROUPS) & jnp.logical_not(is_near(s + 3)))(lambda: dispatch_far(s + 3))
         return carry
 
-    lax.fori_loop(0, GROUPS + 5, step, 0)
+    lax.fori_loop(0, GROUPS + 6, step, 0)
     out[...] = total[...].reshape(TOKENS, OWN).astype(BF16)
 
     def span_of(count):
@@ -602,8 +624,9 @@
     sent(span_of(40), send_sem.at[2])
     sent(span_of(40), send_sem.at[3])
     sent(span_of(40), send_sem.at[4])
-    sent(span_of(20), send_sem.at[5])
-    sent(span_of(20), send_sem.at[6])
+    sent(span_of(16), send_sem.at[5])
+    sent(span_of(16), send_sem.at[6])
+    sent(span_of(8), send_sem.at[18])
     sent(span_of(32), send_sem.at[7])
     sent(span_of(32), send_sem.at[8])
     sent(span_of(64), send_sem.at[9])
@@ -672,7 +695,7 @@
             pltpu.VMEM(blocks, BF16),
             pltpu.VMEM((SIDE, SIDE, OWN), F32),
             pltpu.SemaphoreType.DMA((9,)),
-            pltpu.SemaphoreType.DMA((18,)),
+            pltpu.SemaphoreType.DMA((19,)),
             pltpu.SemaphoreType.DMA((3,)),
             pltpu.SemaphoreType.DMA((10,)),
         ]

time: 116 us -> 110 us (0.948)
  Pallas kernels: 114 us -> 108 us
    pallas_call x1, Pallas kernels: 114 us -> 108 us  [shards(): pl.pallas_call(kernel, out_shape=jax.ShapeDtypeStruct((TOKENS, OWN), BF16...]
where the time goes in v3:
time: 110 us; the launch traced here: 109 us
  Pallas kernels  108 us (98%)
  local copies, waits for them, and re-layouts  1.87 us (2%)
    pallas_call x1, Pallas kernels, shards(): pl.pallas_call(kernel, out_shape=jax.ShapeDtypeStruct((TOKENS, OWN), BF16...  108 us

profile of v3, /device:TPU:1, one launch (start us, length us, event | category | flops | bytes accessed | tf_op | source)
XLA Modules:
  0.0 109.5 jit_solution(8832648182559093154)
XLA Ops:
  0.0 107.6 %shard_map.91 = bf16[1024,256]{1,0:T(8,128)(2,1)} custom-call(bf16[1024,256]{1,0:T(8,128)(2,1)} %pixels.1, f32[9,256]{1,0:T(8,128)} %conv_weight.1, f32[1,1024]{1,0:T(1,128)} %bitcast.3, bf16[1,1024]{1,0:T(2,128)(2,1)} %bitcast.4, s32[1,1024]{1,0:T(1,128)} %bitcast.5, s32[1,8]{1,0:T(1,128)} %table.1, bf16[1,1024,1024]{2,1,0:T(8,128)(2,1)} %gate_hbm.1, ...), custom_call_target="tpu_custom_call" | custom-call | tf_op jit(solution)/shard_map/pallas_call | solution.py:657
  107.6 1.9 %copy.11 = bf16[1024,256]{1,0:T(8,128)(2,1)} copy(bf16[1024,256]{1,0:T(8,128)(2,1)} %shard_map.91) | data formatting | bytes 1048576

commit v4 on v3

--- a/solution.py
+++ b/solution.py
@@ -656,7 +656,7 @@
     per_group = pltpu.SemaphoreType.DMA((GROUPS,))
     return pl.pallas_call(
         kernel,
-        out_shape=jax.ShapeDtypeStruct((TOKENS, OWN), BF16),
+        out_shape=pltpu.VMEM((TOKENS, OWN), BF16),
         in_specs=[hbm] * 9,
         out_specs=vmem,
         scratch_shapes=[
@@ -701,7 +701,7 @@
         ]
         + [per_group] * 10,
         compiler_params=pltpu.CompilerParams(
-            collective_id=0, has_side_effects=True, vmem_limit_bytes=63 * 1024 * 1024
+            collective_id=0, has_side_effects=True, vmem_limit_bytes=56 * 1024 * 1024
         ),
     )(
         pixels,

time: 110 us -> 108 us (0.982)
  no operation moved by 1% of the time
where the time goes in v4:
time: 108 us; the launch traced here: 107 us
  Pallas kernels  107 us (99%)
    pallas_call x1, Pallas kernels, shards(): pl.pallas_call(kernel, out_shape=pltpu.VMEM((TOKENS, OWN), BF16), in_spec...  107 us

profile of v4, /device:TPU:1, one launch (start us, length us, event | category | flops | bytes accessed | tf_op | source)
XLA Modules:
  0.0 107.5 jit_solution(8193229005121875421)
XLA Ops:
  0.0 106.7 %shard_map.91 = bf16[1024,256]{1,0:T(8,128)(2,1)S(1)} custom-call(bf16[1024,256]{1,0:T(8,128)(2,1)} %pixels.1, f32[9,256]{1,0:T(8,128)} %conv_weight.1, f32[1,1024]{1,0:T(1,128)} %bitcast.3, bf16[1,1024]{1,0:T(2,128)(2,1)} %bitcast.4, s32[1,1024]{1,0:T(1,128)} %bitcast.5, s32[1,8]{1,0:T(1,128)} %table.1, bf16[1,1024,1024]{2,1,0:T(8,128)(2,1)} %gate_hbm.1, ...), custom_call_target="tpu_custom_call" | custom-call | tf_op jit(solution)/shard_map/pallas_call | solution.py:657
  106.7 0.8 copy.11

commit v5 on v4

--- a/solution.py
+++ b/solution.py
@@ -606,8 +606,9 @@
         pl.when(s == 0)(conv_complete)
         pl.when((s >= 2) & (s < GROUPS + 2))(lambda: expert(s - 2))
         pl.when((s >= 3) & (s < GROUPS + 3))(lambda: relay(s - 3))
+        pl.when((s >= GROUPS + 2) & (s < GROUPS + 4))(lambda: give_back(s - 4))
         pl.when((s >= 6) & (s < GROUPS + 6))(lambda: combine(s - 6))
-        pl.when((s >= 4) & (s < GROUPS + 4))(lambda: give_back(s - 4))
+        pl.when((s >= 4) & (s < GROUPS + 2))(lambda: give_back(s - 4))
         pl.when((s + 3 < GROUPS) & is_near(s + 3))(lambda: dispatch_near(s + 3))
         pl.when((s + 3 < GROUPS) & jnp.logical_not(is_near(s + 3)))(lambda: dispatch_far(s + 3))
         return carry

time: 108 us -> 108 us (level)
  no operation moved by 1% of the time
where the time goes in v5:
time: 108 us
  Pallas kernels  107 us (99%)
    pallas_call x1, Pallas kernels, shards(): pl.pallas_call(kernel, out_shape=pltpu.VMEM((TOKENS, OWN), BF16), in_spec...  107 us

profile of v5, /device:TPU:1, one launch (start us, length us, event | category | flops | bytes accessed | tf_op | source)
XLA Modules:
  0.0 107.5 jit_solution(1344660739437805050)
XLA Ops:
  0.0 106.7 %shard_map.91 = bf16[1024,256]{1,0:T(8,128)(2,1)S(1)} custom-call(bf16[1024,256]{1,0:T(8,128)(2,1)} %pixels.1, f32[9,256]{1,0:T(8,128)} %conv_weight.1, f32[1,1024]{1,0:T(1,128)} %bitcast.3, bf16[1,1024]{1,0:T(2,128)(2,1)} %bitcast.4, s32[1,1024]{1,0:T(1,128)} %bitcast.5, s32[1,8]{1,0:T(1,128)} %table.1, bf16[1,1024,1024]{2,1,0:T(8,128)(2,1)} %gate_hbm.1, ...), custom_call_target="tpu_custom_call" | custom-call | tf_op jit(solution)/shard_map/pallas_call | solution.py:658
  106.7 0.8 copy.11
